TPU v7x, 256 devices: a whole 4x4x8 slice. The times are simulated.
256 devices in a mesh: ctx: 64 (over x, z, core), fsdp: 4 (over y).
Axes of the slice: x: 4, y: 4, z: 8, core: 2. Of those that a mesh axis runs over, the one named last changes fastest.
Arguments:
- tokens: bfloat16 [4, 8192, 4096], P('fsdp', 'ctx'), may hold values from -48 to 48
- w_query: bfloat16 [4096, 2048], P(('ctx', 'fsdp')), may hold values from -0.09375 to 0.09375
- w_key: bfloat16 [4096, 512], P(('ctx', 'fsdp')), may hold values from -0.09375 to 0.09375
- w_value: bfloat16 [4096, 512], P(('ctx', 'fsdp')), may hold values from -0.09375 to 0.09375
- doc_starts: int32 [4, 71], P('fsdp'), may hold values from 0 to 8192, as said below
- crossing: int32 [4, 64, 7], P('fsdp', 'ctx'), may hold values from 0 to 1, as said below
Outputs:
- attended: bfloat16 [4, 8192, 2048], P('fsdp', 'ctx')
Inputs may be any that keep to these rules, and one draw needn't show every extreme that they name: `doc_starts`: each row begins with 0 and rises strictly through the starts of the sequence's documents, then holds 8192 in the remaining slots; every document holds 1 to 896 tokens, and one document of every sequence holds exactly 896. crossing[q, s, k - 1] is 1 exactly when shard s - k of sequence q exists and holds a token of the document that contains the first token of shard s.
All inputs are finite; a program needn't handle non-finite values.
Results may differ from a plain program's by a relative error of at most 0.023.
Values may be sent and summed in bfloat16 or wider, within the bound.
A program may use at most 128 MiB of HBM per device.

v0:
```python
import jax
import jax.numpy as jnp
from jax import lax
from jax.sharding import PartitionSpec as P

HD = 128


theta_base = 500000.0


def from_behind(array, axis, by):
    count = lax.axis_size(axis)
    pairs = [(i, i + by) for i in range(count) if 0 <= i + by < count]
    return lax.ppermute(array, axis, pairs)


def rotate(vectors, positions):
    half_dim = vectors.shape[-1] // 2
    frequency = theta_base ** (-(jnp.arange(half_dim, dtype=jnp.float32) * 2.0) / vectors.shape[-1])
    angles = positions.astype(jnp.float32)[:, None] * frequency[None, :]
    cos_table = jnp.cos(angles)[:, None, :]
    sin_table = jnp.sin(angles)[:, None, :]
    lower_half = vectors[..., :half_dim]
    upper_half = vectors[..., half_dim:]
    return jnp.concatenate(
        [
            lower_half * cos_table - upper_half * sin_table,
            upper_half * cos_table + lower_half * sin_table,
        ],
        axis=-1,
    )


def doc_index(positions, doc_begin):
    return jnp.sum((doc_begin[None, :] <= positions[:, None]).astype(jnp.int32), axis=1) - 1


def allowed(query_at, key_at, doc_begin, crossed, shard_index, row_count, reach_count):
    query_doc = doc_index(query_at, doc_begin)
    key_doc = doc_index(key_at, doc_begin)
    distance = shard_index - jnp.floor_divide(key_at, row_count)
    picked = crossed[jnp.clip(distance - 1, 0, reach_count - 1)]
    opened = jnp.where(distance == 0, 1, jnp.where(distance > reach_count, 0, picked))
    causal = key_at[None, :] <= query_at[:, None]
    return (
        causal
        & (key_at >= 0)[None, :]
        & (query_doc[:, None] == key_doc[None, :])
        & (opened == 1)[None, :]
    )


def softmax_rows(scores, allowed_map):
    masked = jnp.where(allowed_map, scores, -1e30)
    highest = jnp.max(masked, axis=-1, keepdims=True)
    raised = jnp.where(allowed_map, jnp.exp(masked - highest), 0.0)
    return (raised / jnp.sum(raised, axis=-1, keepdims=True)).astype(jnp.bfloat16)


def score_block(query_block, key_piece, scaling):
    return (
        lax.dot_general(
            query_block, key_piece, (((1,), (1,)), ((), ())), preferred_element_type=jnp.float32
        )
        * scaling
    )


def local(tokens, w_query, w_key, w_value, doc_starts, crossing):
    row_count = tokens.shape[1]
    model_width = tokens.shape[2]
    inputs = tokens.reshape(row_count, model_width)
    doc_begin = doc_starts[0]
    crossed = crossing[0, 0]
    reach_count = crossed.shape[0]
    head_count = w_query.shape[1] // HD
    kv_count = w_key.shape[1] // HD
    group_size = head_count // kv_count
    key_width = kv_count * HD
    scaling = HD ** (-0.5)
    pieces = (
        lax.all_gather(w_query, ("ctx", "fsdp"), axis=0, tiled=True),
        lax.all_gather(w_key, ("ctx", "fsdp"), axis=0, tiled=True),
        lax.all_gather(w_value, ("ctx", "fsdp"), axis=0, tiled=True),
    )
    queries, key_proj, value_proj = tuple(
        (jnp.dot(inputs, piece, preferred_element_type=jnp.float32) for piece in pieces)
    )
    shard_index = lax.axis_index("ctx")
    positions = shard_index * row_count + jnp.arange(row_count, dtype=jnp.int32)
    query_rot = rotate(queries.reshape(row_count, head_count, HD), positions).astype(jnp.bfloat16)
    key_rot = (
        rotate(key_proj.reshape(row_count, kv_count, HD), positions)
        .astype(jnp.bfloat16)
        .reshape(row_count, key_width)
    )
    value_rows = value_proj.astype(jnp.bfloat16)
    own_block = jnp.concatenate([key_rot, value_rows], axis=1)
    blocks = [own_block]
    for distance in range(1, reach_count + 1):
        blocks.insert(0, from_behind(own_block, "ctx", distance))
    window = jnp.concatenate(blocks, axis=0)
    window_rows = (reach_count + 1) * row_count
    key_at = (shard_index - reach_count) * row_count + jnp.arange(window_rows, dtype=jnp.int32)
    allowed_map = allowed(
        positions, key_at, doc_begin, crossed, shard_index, row_count, reach_count
    )
    query_heads = jnp.transpose(query_rot, (1, 0, 2))
    key_heads = jnp.transpose(window[:, :key_width].reshape(window_rows, kv_count, HD), (1, 0, 2))
    value_heads = jnp.transpose(window[:, key_width:].reshape(window_rows, kv_count, HD), (1, 0, 2))

    def one_head(head_index):
        query_block = lax.dynamic_index_in_dim(query_heads, head_index, 0, keepdims=False)
        kv_index = head_index // group_size
        key_block = lax.dynamic_index_in_dim(key_heads, kv_index, 0, keepdims=False)
        value_block = lax.dynamic_index_in_dim(value_heads, kv_index, 0, keepdims=False)
        scores = score_block(query_block, key_block, scaling)
        attention = softmax_rows(scores, allowed_map)
        return jnp.dot(attention, value_block, preferred_element_type=jnp.float32).astype(
            jnp.bfloat16
        )

    context_heads = lax.map(one_head, jnp.arange(head_count, dtype=jnp.int32))
    context = jnp.transpose(context_heads, (1, 0, 2)).reshape(row_count, head_count * HD)
    return context.reshape(1, row_count, head_count * HD)


def solution(mesh):
    return jax.shard_map(
        local,
        mesh=mesh,
        in_specs=(
            P("fsdp", "ctx", None),
            P(("ctx", "fsdp"), None),
            P(("ctx", "fsdp"), None),
            P(("ctx", "fsdp"), None),
            P("fsdp", None),
            P("fsdp", "ctx", None),
        ),
        out_specs=P("fsdp", "ctx", None),
        check_vma=False,
    )
```

profile of v0, /device:TPU:192, one launch (start us, length us, event | category | flops | bytes accessed | tf_op | source)
XLA Modules:
  0.0 540.6 jit_solution(4626073393617494732)
XLA Ops:
  8.8 1.6 fusion.30
  10.4 4.3 compare_select_fusion.1
  15.7 109.0 %all-gather.6.cloned.1.call-done = bf16[4096,512]{1,0:T(8,128)(2,1)} async-done(((bf16[16,512]{1,0:T(8,128)(2,1)}), bf16[4096,512]{1,0:T(8,128)(2,1)}) %all-gather.6.cloned.1.call-update) | async-done | bytes 4194320 | tf_op jit(solution)/shard_map/all_gather | solution.py:84
  124.7 6.4 %copy.22 = bf16[512,4096]{1,0:T(8,128)(2,1)} copy(bf16[512,4096]{0,1:T(8,128)(2,1)} %bitcast.76) | data formatting | bytes 8388608 | tf_op jit(solution)/shard_map/dot_general | solution.py:88
  131.1 3.4 fusion.18
  134.7 106.0 %all-gather.8.cloned.1.call-done = bf16[4096,512]{1,0:T(8,128)(2,1)} async-done(((bf16[16,512]{1,0:T(8,128)(2,1)}), bf16[4096,512]{1,0:T(8,128)(2,1)}) %all-gather.8.cloned.1.call-update) | async-done | bytes 4194320 | tf_op jit(solution)/shard_map/all_gather | solution.py:85
  240.7 2.9 convolution_convert_fusion.1
  243.7 4.8 collective-permute-start
  248.6 5.0 collective-permute-start.2
  253.6 3.7 collective-permute-start.1
  257.4 1.9 collective-permute-start.6
  259.3 4.4 collective-permute-start.5
  263.7 2.4 collective-permute-done
  266.1 7.7 %collective-permute-start.3 = (bf16[128,1024]{1,0:T(8,128)(2,1)S(1)}, bf16[128,1024]{1,0:T(8,128)(2,1)S(1)}, u32[]{:S(2)}, u32[]{:S(2)}) collective-permute-start(bf16[128,1024]{1,0:T(8,128)(2,1)S(1)} %pad_maximum_fusion), channel_id=1, source_target_pairs={{0,16},{4,20},{8,24},{12,28},{16,32},{20,36},{24,40},{28,44},{32,4... | collective-permute-start | bytes 786440 | tf_op jit(solution)/shard_map/ppermute | solution.py:15
  273.8 24.5 %collective-permute-done.1 = bf16[128,1024]{1,0:T(8,128)(2,1)S(1)} collective-permute-done((bf16[128,1024]{1,0:T(8,128)(2,1)S(1)}, bf16[128,1024]{1,0:T(8,128)(2,1)S(1)}, u32[]{:S(2)}, u32[]{:S(2)}) %collective-permute-start.1) | collective-permute-done | bytes 262176 | tf_op jit(solution)/shard_map/ppermute | solution.py:15
  298.3 3.2 collective-permute-start.4
  301.6 5.6 %collective-permute-done.3 = bf16[128,1024]{1,0:T(8,128)(2,1)S(1)} collective-permute-done((bf16[128,1024]{1,0:T(8,128)(2,1)S(1)}, bf16[128,1024]{1,0:T(8,128)(2,1)S(1)}, u32[]{:S(2)}, u32[]{:S(2)}) %collective-permute-start.3) | collective-permute-done | bytes 262176 | tf_op jit(solution)/shard_map/ppermute | solution.py:15
  307.2 20.6 %collective-permute-done.4 = bf16[128,1024]{1,0:T(8,128)(2,1)S(1)} collective-permute-done((bf16[128,1024]{1,0:T(8,128)(2,1)S(1)}, bf16[128,1024]{1,0:T(8,128)(2,1)S(1)}, u32[]{:S(2)}, u32[]{:S(2)}) %collective-permute-start.4) | collective-permute-done | bytes 262176 | tf_op jit(solution)/shard_map/ppermute | solution.py:15
  328.8 59.9 %all-gather.4.cloned.1.call-done = bf16[4096,2048]{1,0:T(8,128)(2,1)} async-done(((bf16[16,2048]{1,0:T(8,128)(2,1)}), bf16[4096,2048]{1,0:T(8,128)(2,1)}) %all-gather.4.cloned.1.call-update) | async-done | bytes 16777232 | tf_op jit(solution)/shard_map/all_gather | solution.py:83
  388.7 20.7 %copy.21 = bf16[2048,4096]{1,0:T(8,128)(2,1)} copy(bf16[2048,4096]{0,1:T(8,128)(2,1)} %bitcast.74) | data formatting | bytes 33554432 | tf_op jit(solution)/shard_map/dot_general | solution.py:88
  409.3 8.1 %fusion.20 = f32[128,16,128]{0,2,1:T(8,128)S(1)} fusion(bf16[16,128,4096]{2,1,0:T(8,128)(2,1)} %bitcast.73, bf16[1,128,4096]{2,1,0:T(8,128)(2,1)S(1)} %copy-done), kind=kOutput, calls=%fused_computation.29 | convolution fusion | flops 2147483648 | bytes 18874368 | tf_op jit(solution)/shard_map/dot_general | solution.py:88
  418.4 113.2 %while.13 = (s32[]{:T(128)}, bf16[16,128,128]{2,1,0:T(8,128)(2,1)}, s32[16]{0:T(128)S(1)}, bf16[16,128,128]{1,2,0:T(8,128)(2,1)}, bf16[4,1024,128]{2,1,0:T(8,128...) while((s32[]{:T(128)}, bf16[16,128,128]{2,1,0:T(8,128)(2,1)}, ...), condition=%wide.region_5.6_spmd.clone, body=%wide.region_2.5_spmd.clone.sunk | while | flops 70401808 | bytes 2199458 | solution.py:124
  422.9 1.2 fusion.39
  430.0 1.2 fusion.39
  437.0 1.2 fusion.39
  451.2 1.2 fusion.39
  465.3 1.2 fusion.39
  479.5 1.2 fusion.39
  493.6 1.2 fusion.39
  507.8 1.2 fusion.39
  521.9 1.2 fusion.39
  531.6 1.4 copy.27
  (97 shorter events, 48.1 us)
Async XLA Ops:
  6.5 124.5 %copy-start = (bf16[1,128,4096]{2,1,0:T(8,128)(2,1)S(1)}, bf16[1,128,4096]{2,1,0:T(8,128)(2,1)}, u32[]{:S(2)}) copy-start(bf16[1,128,4096]{2,1,0:T(8,128)(2,1)} %param.8) | copy-start | bytes 3145732
  6.5 118.1 %all-gather.6.cloned.1.call-start = ((), (), s32[]{:S(2)}) async-start(), calls=%async_computation.1 | async-start | bytes 4210688 | tf_op jit(solution)/shard_map/all_gather | solution.py:84
  7.3 233.5 %all-gather.8.cloned.1.call-start = ((), (), s32[]{:S(2)}) async-start(), calls=%async_computation.2 | async-start | bytes 4210688 | tf_op jit(solution)/shard_map/all_gather | solution.py:85
  8.0 380.6 %all-gather.4.cloned.1.call-start = ((), (), s32[]{:S(2)}) async-start(), calls=%async_computation | async-start | bytes 16842752 | tf_op jit(solution)/shard_map/all_gather | solution.py:83
  134.7 113.8 %copy-start.1 = (s32[1,71]{1,0:T(1,128)S(1)}, s32[1,71]{1,0:T(1,128)}, u32[]{:S(2)}) copy-start(s32[1,71]{1,0:T(1,128)} %param.12) | copy-start | bytes 856
  243.7 22.4 %collective-permute-start = (bf16[128,1024]{1,0:T(8,128)(2,1)S(1)}, bf16[128,1024]{1,0:T(8,128)(2,1)S(1)}, u32[]{:S(2)}, u32[]{:S(2)}) collective-permute-start(bf16[128,1024]{1,0:T(8,128)(2,1)S(1)} %pad_maximum_fusion), channel_id=1, source_target_pairs={{0,28},{4,32},{8,36},{12,40},{16,44},{20,48},{24,52},{28,56},{32,6... | collective-permute-start | bytes 786440 | tf_op jit(solution)/shard_map/ppermute | solution.py:15
  248.6 52.9 %collective-permute-start.2 = (bf16[128,1024]{1,0:T(8,128)(2,1)S(1)}, bf16[128,1024]{1,0:T(8,128)(2,1)S(1)}, u32[]{:S(2)}, u32[]{:S(2)}) collective-permute-start(bf16[128,1024]{1,0:T(8,128)(2,1)S(1)} %pad_maximum_fusion), channel_id=1, source_target_pairs={{0,20},{4,24},{8,28},{12,32},{16,36},{20,40},{24,44},{28,48},{32,5... | collective-permute-start | bytes 786440 | tf_op jit(solution)/shard_map/ppermute | solution.py:15
  253.6 44.7 %collective-permute-start.1 = (bf16[128,1024]{1,0:T(8,128)(2,1)S(1)}, bf16[128,1024]{1,0:T(8,128)(2,1)S(1)}, u32[]{:S(2)}, u32[]{:S(2)}) collective-permute-start(bf16[128,1024]{1,0:T(8,128)(2,1)S(1)} %pad_maximum_fusion), channel_id=1, source_target_pairs={{0,24},{4,28},{8,32},{12,36},{16,40},{20,44},{24,48},{28,52},{32,5... | collective-permute-start | bytes 786440 | tf_op jit(solution)/shard_map/ppermute | solution.py:15
  257.4 70.6 %collective-permute-start.6 = (bf16[128,1024]{1,0:T(8,128)(2,1)S(1)}, bf16[128,1024]{1,0:T(8,128)(2,1)S(1)}, u32[]{:S(2)}, u32[]{:S(2)}) collective-permute-start(bf16[128,1024]{1,0:T(8,128)(2,1)S(1)} %pad_maximum_fusion), channel_id=1, source_target_pairs={{0,4},{4,8},{8,12},{12,16},{16,20},{20,24},{24,28},{28,32},{32,36}... | collective-permute-start | bytes 786440 | tf_op jit(solution)/shard_map/ppermute | solution.py:15
  259.3 68.6 %collective-permute-start.5 = (bf16[128,1024]{1,0:T(8,128)(2,1)S(1)}, bf16[128,1024]{1,0:T(8,128)(2,1)S(1)}, u32[]{:S(2)}, u32[]{:S(2)}) collective-permute-start(bf16[128,1024]{1,0:T(8,128)(2,1)S(1)} %pad_maximum_fusion), channel_id=1, source_target_pairs={{0,8},{4,12},{8,16},{12,20},{16,24},{20,28},{24,32},{28,36},{32,40... | collective-permute-start | bytes 786440 | tf_op jit(solution)/shard_map/ppermute | solution.py:15
  266.1 41.1 %collective-permute-start.3 = (bf16[128,1024]{1,0:T(8,128)(2,1)S(1)}, bf16[128,1024]{1,0:T(8,128)(2,1)S(1)}, u32[]{:S(2)}, u32[]{:S(2)}) collective-permute-start(bf16[128,1024]{1,0:T(8,128)(2,1)S(1)} %pad_maximum_fusion), channel_id=1, source_target_pairs={{0,16},{4,20},{8,24},{12,28},{16,32},{20,36},{24,40},{28,44},{32,4... | collective-permute-start | bytes 786440 | tf_op jit(solution)/shard_map/ppermute | solution.py:15
  298.3 29.6 %collective-permute-start.4 = (bf16[128,1024]{1,0:T(8,128)(2,1)S(1)}, bf16[128,1024]{1,0:T(8,128)(2,1)S(1)}, u32[]{:S(2)}, u32[]{:S(2)}) collective-permute-start(bf16[128,1024]{1,0:T(8,128)(2,1)S(1)} %pad_maximum_fusion), channel_id=1, source_target_pairs={{0,12},{4,16},{8,20},{12,24},{16,28},{20,32},{24,36},{28,40},{32,4... | collective-permute-start | bytes 786440 | tf_op jit(solution)/shard_map/ppermute | solution.py:15
Sparse Core Ops, SparseCore 0:
  11.1 113.5 all-gather.5
  128.4 112.3 all-gather.7
  244.3 144.2 all-gather.3
where the time goes:
time: 549 us; the launch traced here: 541 us
  waiting for transfers between devices  330 us (60%)
  loops' own time  61 us (11%)
  matrix products  49.9 us (9%)
  local copies, waits for them, and re-layouts  42.4 us (8%)
  starting transfers between devices  30.9 us (6%)
  between operations  13.4 us (2%)
  other arithmetic  12.9 us (2%)
    all_gather x1, waiting for transfers between devices, local(): lax.all_gather(w_key, ('ctx', 'fsdp'), axis=0, tiled=True)  109 us
    all_gather x1, waiting for transfers between devices, local(): lax.all_gather(w_value, ('ctx', 'fsdp'), axis=0, tiled=True)  106 us
    another operation x1, loops' own time, local(): context_heads = lax.map(one_head, jnp.arange(head_count, dtype=jnp.int32))  61 us
    all_gather x1, waiting for transfers between devices, local(): lax.all_gather(w_query, ('ctx', 'fsdp'), axis=0, tiled=True)  59.9 us
    ppermute x7, waiting for transfers between devices, from_behind(): return lax.ppermute(array, axis, pairs)  53.1 us
    ppermute x7, starting transfers between devices, from_behind(): return lax.ppermute(array, axis, pairs)  30.8 us
    dot_general x2, local copies, waits for them, and re-layouts, local(): jnp.dot(inputs, piece, preferred_element_type=jnp.float32)  27.1 us
    dot_general x16, matrix products, score_block(): lax.dot_general(query_block, key_piece, (((1,), (1,)), ((), ())), preferr...  18.6 us
  transfers between devices with their start and end apart: 10, of which 7 were waited for; matrix products, arithmetic and copies ran while one was open for 4% of the time, Pallas kernels for 0%

commit v1 on v0

v1 whole, which is shorter than its diff:
```python
import functools

import jax
import jax.numpy as jnp
import numpy as np
from jax import lax
from jax.experimental import pallas as pl
from jax.experimental.pallas import tpu as pltpu
from jax.sharding import PartitionSpec as P

MESH = pl.DeviceIdType.MESH
NX, NY, NZ = 4, 4, 8
ROWS = 128
D = 4096
HD = 128
GROUP = 4
REACH = 7
QC = GROUP * HD
COLS = 2 * HD + QC
WINDOW = (REACH + 1) * ROWS
OFFSETS = (0, 1, 3, 2)
SLOT_OF = {0: 0, 1: 1, 3: 2, 2: 3}
THETA = 500000.0
SCALE = HD ** -0.5
NEG = -1e30


def tables():
    freq = THETA ** (-(np.arange(HD // 2) * 2.0) / HD)
    freq = np.concatenate([freq, freq])
    rows = np.arange(ROWS)[:, None] * freq[None, :]
    shards = (np.arange(NX * NZ * 2) * ROWS)[:, None] * freq[None, :]
    row_tab = np.stack([np.cos(rows), np.sin(rows)]).astype(np.float32)
    shard_tab = np.stack([np.cos(shards), np.sin(shards)], axis=1).astype(np.float32)
    return row_tab, shard_tab


def kernel(
    tok_in, wq_in, wk_in, wv_in, starts, opened, row_tab, shard_tab,
    out,
    tok, w, kv, q, att, opens,
    loc_sem, tok_s, tok_r, a_s, a_r, z_s, z_r, y_s, y_r, c_s, c_r, h_s, h_r, hc_s, hc_r, o_s, o_r,
):
    ctx = lax.axis_index("ctx")
    y = lax.axis_index("fsdp")
    x = ctx // (2 * NZ)
    z = lax.rem(ctx // 2, NZ)
    c = lax.rem(ctx, 2)
    o = 1 - c

    def dev(px, py, pz, pc):
        return ((px * NZ + pz) * 2 + pc, py)

    def xs(k):
        return lax.rem(x + k + NX, NX)

    def ys(k):
        return lax.rem(y + k + NY, NY)

    def zs(k):
        return lax.rem(z + k + NZ, NZ)

    sibling = dev(x, y, z, o)
    peers = [dev(xs(k), y, z, c) for k in (1, 2, 3)]
    peers += [dev(x, ys(k), z, c) for k in (1, 2, 3)]
    peers += [dev(x, y, zs(k), c) for k in range(1, NZ)]
    peers += [sibling, dev(x, y, zs(1), o), dev(x, y, zs(-1), o)]

    sent = []

    def send(src, dst, ssem, rsem, to):
        cp = pltpu.make_async_remote_copy(
            src_ref=src, dst_ref=dst, send_sem=ssem, recv_sem=rsem, device_id=to, device_id_type=MESH
        )
        cp.start()
        sent.append(cp)
        return cp

    def arrive(dst, ssem, rsem):
        pltpu.make_async_remote_copy(
            src_ref=dst, dst_ref=dst, send_sem=ssem, recv_sem=rsem, device_id=sibling, device_id_type=MESH
        ).wait_recv()

    local = []

    def move(src, dst, sem):
        cp = pltpu.make_async_copy(src, dst, sem)
        cp.start()
        local.append(cp)
        return cp

    own_tok = move(tok_in, tok.at[0], loc_sem.at[0])
    own_open = move(opened, opens.at[0], loc_sem.at[1])
    row16 = c * 64 + y * 16
    parts = ((wk_in, HD, 0), (wv_in, HD, HD), (wq_in, QC, 2 * HD))
    own_w = [
        move(
            ref.at[:, pl.ds(pl.multiple_of(x * n, n), n)],
            w.at[x, z, pl.ds(row16, 16), pl.ds(at, n)],
            loc_sem.at[2 + i],
        )
        for i, (ref, n, at) in enumerate(parts)
    ]

    barrier = pltpu.get_barrier_semaphore()
    for peer in peers:
        pl.semaphore_signal(barrier, inc=1, device_id=peer, device_id_type=MESH)
    pl.semaphore_wait(barrier, len(peers))

    for i, (ref, n, at) in enumerate(parts):
        for k in (1, 3, 2):
            to = xs(k)
            send(
                ref.at[:, pl.ds(pl.multiple_of(to * n, n), n)],
                w.at[x, z, pl.ds(row16, 16), pl.ds(at, n)],
                a_s.at[i, k - 1], a_r.at[i, k - 1], dev(to, y, z, c),
            )
    CH = D // 4
    for j in range(4):
        for side, (k, slot, order) in enumerate(((1, 2, (0, 1, 2, 3)), (-1, 1, (2, 3, 0, 1)))):
            cols = pl.ds(order[j] * CH, CH)
            send(
                tok_in.at[:, cols], tok.at[slot, :, cols],
                tok_s.at[side, order[j]], tok_r.at[slot - 1, order[j]], dev(xs(k), y, z, c),
            )
    for k in (1, 3, 2):
        slot = SLOT_OF[(-k) % NX]
        send(opened, opens.at[slot], a_s.at[3, k - 1], a_r.at[3, slot - 1], dev(xs(k), y, z, c))

    groups = ((0, 2 * HD), (2 * HD, QC))

    def block(g, px, pz):
        at, n = groups[g]
        return w.at[px, pz, pl.ds(row16, 16), pl.ds(at, n)]

    def zline(g, py, pc, half=None):
        at, n = groups[g]
        rows = pl.ds(pc * 64 + py * 16, 16)
        if half is None:
            return w.at[:, :, rows, pl.ds(at, n)]
        return w.at[pl.ds(2 * half, 2), :, rows, pl.ds(at, n)]

    def zblock(g, pz):
        at, n = groups[g]
        return w.at[:, pz, pl.ds(row16, 16), pl.ds(at, n)]

    def stage_z(g):
        for i in (0, 1) if g == 0 else (2,):
            ref, n, at = parts[i]
            own_w[i].wait()
            for k in (1, 3, 2):
                src = xs(-k)
                arrive(w.at[src, z, pl.ds(row16, 16), pl.ds(at, n)], a_s.at[i, k - 1], a_r.at[i, k - 1])
        for k in (1, 7, 2, 6, 3, 5, 4):
            send(zblock(g, z), zblock(g, z), z_s.at[g, k - 1], z_r.at[g, k - 1], dev(x, y, zs(k), c))

    def stage_y(g):
        for k in (1, 7, 2, 6, 3, 5, 4):
            arrive(zblock(g, zs(-k)), z_s.at[g, k - 1], z_r.at[g, k - 1])
        for j in range(2):
            for side, k in enumerate((1, -1)):
                half = j if side == 0 else 1 - j
                line = zline(g, y, c, half)
                send(line, line, y_s.at[g, side, half], y_r.at[g, side, half], dev(x, ys(k), z, c))
        line = zline(g, y, c)
        send(line, line, c_s.at[g, 0], c_r.at[g, 0], sibling)

    def stage_forward(g):
        for side, k in enumerate((-1, 1)):
            line = zline(g, ys(k), c, side)
            arrive(line, y_s.at[g, side, side], y_r.at[g, side, side])
            send(line, line, y_s.at[g, 2, side], y_r.at[g, 2, side], dev(x, ys(-k), z, c))

    def stage_share(g):
        for side, k in enumerate((-1, 1)):
            arrive(zline(g, ys(k), c, 1 - side), y_s.at[g, side, 1 - side], y_r.at[g, side, 1 - side])
            line = zline(g, ys(k), c)
            send(line, line, c_s.at[g, 1 + side], c_r.at[g, 1 + side], sibling)
        for half in range(2):
            arrive(zline(g, ys(2), c, half), y_s.at[g, 2, half], y_r.at[g, 2, half])
        line = zline(g, ys(2), c)
        send(line, line, c_s.at[g, 3], c_r.at[g, 3], sibling)

    def stage_end(g):
        for i, k in enumerate((0, -1, 1, 2)):
            arrive(zline(g, ys(k), o), c_s.at[g, i], c_r.at[g, i])

    def forward_tokens(j):
        for side, (slot, k) in enumerate(((2, 1), (1, -1))):
            n = 2 * side + j
            cols = pl.ds(n * CH, CH)
            arrive(tok.at[slot, :, cols], tok_s.at[side, n], tok_r.at[slot - 1, n])
            send(tok.at[slot, :, cols], tok.at[3, :, cols], tok_s.at[2, n], tok_r.at[2, n], dev(xs(k), y, z, c))

    stage_z(0)
    stage_z(1)
    stage_y(0)
    forward_tokens(0)
    stage_forward(0)
    forward_tokens(1)
    stage_y(1)
    stage_share(0)
    stage_forward(1)
    stage_end(0)
    for side, slot in enumerate((2, 1)):
        for n in (2 - 2 * side, 3 - 2 * side):
            cols = pl.ds(n * CH, CH)
            arrive(tok.at[slot, :, cols], tok_s.at[side, n], tok_r.at[slot - 1, n])
    own_tok.wait()

    cos_row, sin_row = row_tab[0], row_tab[1]
    sign = jnp.where(lax.broadcasted_iota(jnp.int32, (1, HD), 1) < HD // 2, -1.0, 1.0).astype(jnp.float32)

    def shard_of(p):
        return xs(OFFSETS[p]) * (2 * NZ) + z * 2 + c

    def rotary(p):
        tab = shard_tab[shard_of(p)]
        ca, sa = tab[0:1, :], tab[1:2, :]
        return ca * cos_row - sa * sin_row, (sa * cos_row + ca * sin_row) * sign

    def rotate(v, cs, sn):
        return v * cs + pltpu.roll(v, HD // 2, 1) * sn

    def project(first, count, at, n):
        total = None
        for j in range(4):
            rows = tok[first:first + count, :, j * CH:(j + 1) * CH].reshape(count * ROWS, CH)
            cols = w[j, :, :, at:at + n].reshape(CH, n)
            part = jnp.dot(rows, cols, preferred_element_type=jnp.float32)
            total = part if total is None else total + part
        return total

    wrap = jnp.where(z == NZ - 1, 1, 0)

    def slot_ahead(p):
        turned = SLOT_OF[(OFFSETS[p] + 1) % NX]
        return jnp.where(wrap == 1, turned, p)

    def send_own(p):
        tile = kv.at[p, 8 + c]
        send(tile, tile, hc_s.at[p, 0], hc_r.at[p, 0], sibling)
        n = slot_ahead(p)
        send(tile, kv.at[n, 6 + c], h_s.at[p, 0], h_r.at[n, 0], dev(x, y, zs(1), c))

    def keys(first, count):
        total = project(first, count, 0, 2 * HD)
        for i in range(count):
            p = first + i
            part = total[i * ROWS:(i + 1) * ROWS]
            cs, sn = rotary(p)
            kv[p, 8 + c, :, 0:HD] = rotate(part[:, 0:HD], cs, sn).astype(jnp.bfloat16)
            kv[p, 8 + c, :, HD:2 * HD] = part[:, HD:2 * HD].astype(jnp.bfloat16)
            send_own(p)

    def queries(first, count):
        total = project(first, count, 2 * HD, QC)
        for i in range(count):
            p = first + i
            part = total[i * ROWS:(i + 1) * ROWS]
            cs, sn = rotary(p)
            for h in range(GROUP):
                head = part[:, h * HD:(h + 1) * HD]
                q[p, h] = rotate(head, cs, sn).astype(jnp.bfloat16)

    last = []

    def pass_on(p, d):
        tile = kv.at[p, 2 * (4 - d) + c]
        arrive(tile, h_s.at[p, d - 1], h_r.at[p, d - 1])
        n = slot_ahead(p)
        if d < 3:
            send(tile, kv.at[n, 2 * (3 - d) + c], h_s.at[p, d], h_r.at[n, d], dev(x, y, zs(1), c))
        else:
            cp = pltpu.make_async_remote_copy(
                src_ref=kv.at[p, 3], dst_ref=kv.at[n, 1], send_sem=h_s.at[p, 3], recv_sem=h_r.at[n, 3],
                device_id=dev(x, y, zs(1), 0), device_id_type=MESH,
            )
            last.append(cp)

            @pl.when(c == 1)
            def _():
                cp.start()
        send(tile, tile, hc_s.at[p, d], hc_r.at[p, d], sibling)

    def gather_keys(p):
        for d in range(4):
            arrive(kv.at[p, 2 * (4 - d) + o], hc_s.at[p, d], hc_r.at[p, d])

        @pl.when(c == 0)
        def _():
            arrive(kv.at[p, 1], h_s.at[p, 3], h_r.at[p, 3])

    def attend(p):
        s = shard_of(p)
        q_at = (s * ROWS + lax.broadcasted_iota(jnp.int32, (ROWS, 1), 0)).astype(jnp.float32)
        begin = jnp.max(jnp.where(starts[...] <= q_at, starts[...], 0.0), axis=1, keepdims=True)
        k_at = ((s - REACH) * ROWS + lax.broadcasted_iota(jnp.int32, (1, WINDOW), 1)).astype(jnp.float32)
        k_at = jnp.where(opens[p] == 1, k_at, -1.0)
        seen = (k_at <= q_at) & (k_at >= begin)
        k_all = kv[p, pl.ds(1 + c, 8), :, 0:HD].reshape(WINDOW, HD)
        v_all = kv[p, pl.ds(1 + c, 8), :, HD:2 * HD].reshape(WINDOW, HD)
        for h in range(GROUP):
            scores = lax.dot_general(
                q[p, h], k_all, (((1,), (1,)), ((), ())), preferred_element_type=jnp.float32
            ) * SCALE
            scores = jnp.where(seen, scores, NEG)
            top = jnp.max(scores, axis=1, keepdims=True)
            raised = jnp.exp(scores - top)
            total = jnp.sum(raised, axis=1, keepdims=True)
            mixed = jnp.dot(raised.astype(jnp.bfloat16), v_all, preferred_element_type=jnp.float32)
            att[p, :, h * HD:(h + 1) * HD] = (mixed / total).astype(jnp.bfloat16)
        mine = out.at[:, pl.ds(pl.multiple_of(x * QC, QC), QC)]
        k = OFFSETS[p]
        if k == 0:
            move(att.at[p], mine, loc_sem.at[5])
        else:
            send(att.at[p], mine, o_s.at[k - 1], o_r.at[k - 1], dev(xs(k), y, z, c))

    keys(0, 3)
    stage_share(1)
    for j in range(4):
        cols = pl.ds(j * CH, CH)
        arrive(tok.at[3, :, cols], tok_s.at[2, j], tok_r.at[2, j])
    keys(3, 1)
    stage_end(1)
    for p in (0, 1):
        for d in (1, 2, 3):
            pass_on(p, d)
    queries(0, 3)
    for p in (2, 3):
        for d in (1, 2, 3):
            pass_on(p, d)
    queries(3, 1)
    own_open.wait()
    for slot in (1, 2, 3):
        arrive(opens.at[slot], a_s.at[3, slot - 1], a_r.at[3, slot - 1])
    for p in (1, 0, 2, 3):
        gather_keys(p)
        attend(p)

    for k in (1, 3, 2):
        src = xs(-k)
        arrive(out.at[:, pl.ds(pl.multiple_of(src * QC, QC), QC)], o_s.at[k - 1], o_r.at[k - 1])
    local[-1].wait()
    for cp in sent:
        cp.wait_send()
    for cp in last:
        @pl.when(c == 1)
        def _(cp=cp):
            cp.wait_send()


def local(tokens, w_query, w_key, w_value, doc_starts, crossing):
    row_tab, shard_tab = tables()
    starts = jnp.pad(doc_starts, ((0, 0), (0, HD - doc_starts.shape[1])), constant_values=NX * NZ * 2 * ROWS)
    starts = starts.astype(jnp.float32)
    opened = jnp.concatenate([crossing[0, :, ::-1], jnp.ones((1, 1), jnp.int32)], axis=1)
    opened = jnp.repeat(opened, ROWS, axis=1)
    anyw = pl.BlockSpec(memory_space=pl.ANY)
    vmem = pl.BlockSpec(memory_space=pltpu.VMEM)
    dma = pltpu.SemaphoreType.DMA
    bf16 = jnp.bfloat16
    out = pl.pallas_call(
        kernel,
        out_shape=jax.ShapeDtypeStruct((ROWS, NX * QC), bf16),
        in_specs=[anyw, anyw, anyw, anyw, vmem, vmem, vmem, vmem],
        out_specs=anyw,
        scratch_shapes=[
            pltpu.VMEM((4, ROWS, D), bf16),
            pltpu.VMEM((NX, NZ, ROWS, COLS), bf16),
            pltpu.VMEM((4, 10, ROWS, 2 * HD), bf16),
            pltpu.VMEM((4, GROUP, ROWS, HD), bf16),
            pltpu.VMEM((4, ROWS, QC), bf16),
            pltpu.VMEM((4, 1, WINDOW), jnp.int32),
            dma((6,)),
            dma((3, 4)), dma((3, 4)),
            dma((4, 3)), dma((4, 3)),
            dma((2, 7)), dma((2, 7)),
            dma((2, 3, 2)), dma((2, 3, 2)),
            dma((2, 4)), dma((2, 4)),
            dma((4, 4)), dma((4, 4)),
            dma((4, 4)), dma((4, 4)),
            dma((3,)), dma((3,)),
        ],
        compiler_params=pltpu.CompilerParams(
            collective_id=0, has_side_effects=True, vmem_limit_bytes=48 << 20
        ),
    )(
        tokens.reshape(ROWS, D), w_query, w_key, w_value, starts, opened,
        jnp.asarray(row_tab), jnp.asarray(shard_tab),
    )
    return out.reshape(1, ROWS, NX * QC)


def solution(mesh):
    return jax.shard_map(
        local,
        mesh=mesh,
        in_specs=(
            P("fsdp", "ctx", None),
            P(("ctx", "fsdp"), None),
            P(("ctx", "fsdp"), None),
            P(("ctx", "fsdp"), None),
            P("fsdp", None),
            P("fsdp", "ctx", None),
        ),
        out_specs=P("fsdp", "ctx", None),
        check_vma=False,
    )
```

time: 549 us -> 118 us (0.21); the launches traced: 541 us -> 118 us
  waiting for transfers between devices: 330 us -> 0 us
  Pallas kernels: 0 us -> 110 us
  loops' own time: 61 us -> 0 us
  matrix products: 49.9 us -> 0 us
  local copies, waits for them, and re-layouts: 42.4 us -> 7.51 us
  starting transfers between devices: 30.9 us -> 0 us
  between operations: 13.4 us -> 0.02 us
  other arithmetic: 12.9 us -> 0.08 us
    all_gather x3 -> x0, waiting for transfers between devices: 275 us -> none  [the longest x1 109 us: local(): lax.all_gather(w_key, ('ctx', 'fsdp'), axis=0, tiled=True)]
    pallas_call x0 -> x1, Pallas kernels: none -> 110 us  [local(): pl.pallas_call(kernel, out_shape=jax.ShapeDtypeStruct((ROWS, NX * QC), bf...]
    another operation x1 -> x0, loops' own time: 61 us -> none  [local(): context_heads = lax.map(one_head, jnp.arange(head_count, dtype=jnp.int32))]
    ppermute x7 -> x0, waiting for transfers between devices: 53.1 us -> none  [from_behind(): return lax.ppermute(array, axis, pairs)]
    dot_general x35 -> x0, matrix products: 49.9 us -> none  [the longest x16 18.6 us: score_block(): lax.dot_general(query_block, key_piece, (((1,), (1,)), ((), ())), preferr...]
    ppermute x7 -> x0, starting transfers between devices: 30.8 us -> none  [from_behind(): return lax.ppermute(array, axis, pairs)]
    dot_general x2 -> x0, local copies, waits for them, and re-layouts: 27.1 us -> none  [local(): jnp.dot(inputs, piece, preferred_element_type=jnp.float32)]
    dynamic_slice x16 -> x0, local copies, waits for them, and re-layouts: 10.3 us -> none  [local(): context_heads = lax.map(one_head, jnp.arange(head_count, dtype=jnp.int32))]
  transfers between devices with their start and end apart: 10 -> 0, of which waited for: 7 -> 0; matrix products, arithmetic and copies ran while one was open for 4% -> 0% of each run, Pallas kernels for 0% -> 0%
where the time goes in v1:
time: 118 us
  Pallas kernels  110 us (93%)
  local copies, waits for them, and re-layouts  7.51 us (6%)
    pallas_call x1, Pallas kernels, local(): pl.pallas_call(kernel, out_shape=jax.ShapeDtypeStruct((ROWS, NX * QC), bf...  110 us
    unnamed x17, local copies, waits for them, and re-layouts  7.34 us

profile of v1, /device:TPU:192, one launch (start us, length us, event | category | flops | bytes accessed | tf_op | source)
XLA Modules:
  0.0 118.1 jit_solution(12485627309865614359)
XLA Ops:
  0.0 0.0 copy-start.6
  0.0 0.7 copy-done.6
  0.7 0.0 copy-start.7
  0.7 0.6 copy-done.7
  1.3 0.1 rev.3
  1.4 0.1 add_bitcast_fusion
  1.5 0.1 broadcast_in_dim.5
  1.6 0.0 copy-start
  1.6 1.2 %copy-done = bf16[1,128,4096]{2,1,0:T(8,128)(2,1)S(1)} copy-done((bf16[1,128,4096]{2,1,0:T(8,128)(2,1)S(1)}, bf16[1,128,4096]{2,1,0:T(8,128)(2,1)}, u32[]{:S(2)}) %copy-start) | copy-done | bytes 1048600
  2.8 0.0 copy-start.1
  2.8 0.9 copy-done.1
  3.7 0.0 copy-start.2
  3.7 0.8 copy-done.2
  4.5 0.0 copy-start.3
  4.5 0.8 copy-done.3
  5.4 0.0 copy-start.4
  5.4 0.7 copy-done.4
  6.1 0.0 copy-start.5
  6.1 0.7 copy-done.5
  6.8 110.5 %shard_map.82 = bf16[128,2048]{1,0:T(8,128)(2,1)S(1)} custom-call(bf16[128,4096]{1,0:T(8,128)(2,1)S(1)} %bitcast.7, bf16[16,2048]{1,0:T(8,128)(2,1)S(1)} %copy-done.2, bf16[16,512]{1,0:T(8,128)(2,1)S(1)} %copy-done.4, bf16[16,512]{1,0:T(8,128)(2,1)S(1)} %copy-done.5, f32[1,128]{1,0:T(1,128)S(1)} %pad_convert_fusion.starts, s32[1,1024]{1,0:T(1,128)S(1)} %bitcast.8, ...), custom_call_target="tpu_custom_call" | custom-call | tf_op jit(solution)/shard_map/pallas_call | solution.py:364
  117.3 0.8 copy.10
  (1 shorter events, 0.0 us)
Async XLA Ops:
  0.0 0.7 copy-start.6
  0.7 0.7 copy-start.7
  1.6 1.2 %copy-start = (bf16[1,128,4096]{2,1,0:T(8,128)(2,1)S(1)}, bf16[1,128,4096]{2,1,0:T(8,128)(2,1)}, u32[]{:S(2)}) copy-start(bf16[1,128,4096]{2,1,0:T(8,128)(2,1)} %param.8) | copy-start | bytes 3145732
  2.8 0.9 copy-start.1
  3.7 0.8 copy-start.2
  4.5 0.8 copy-start.3
  5.4 0.7 copy-start.4
  6.1 0.7 copy-start.5

commit v2 on v1

--- a/solution.py
+++ b/solution.py
@@ -28,17 +28,15 @@
 def tables():
     freq = THETA ** (-(np.arange(HD // 2) * 2.0) / HD)
     freq = np.concatenate([freq, freq])
-    rows = np.arange(ROWS)[:, None] * freq[None, :]
-    shards = (np.arange(NX * NZ * 2) * ROWS)[:, None] * freq[None, :]
-    row_tab = np.stack([np.cos(rows), np.sin(rows)]).astype(np.float32)
-    shard_tab = np.stack([np.cos(shards), np.sin(shards)], axis=1).astype(np.float32)
-    return row_tab, shard_tab
+    at = np.concatenate([np.arange(ROWS), np.arange(NX * NZ * 2) * ROWS])
+    angles = at[:, None] * freq[None, :]
+    return np.stack([np.cos(angles), np.sin(angles)]).astype(np.float32)
 
 
 def kernel(
-    tok_in, wq_in, wk_in, wv_in, starts, opened, row_tab, shard_tab,
+    tok_in, wq_in, wk_in, wv_in, starts_in, crossing, tab_in,
     out,
-    tok, w, kv, q, att, opens,
+    tok, w, kv, q, att, opens, tab, starts,
     loc_sem, tok_s, tok_r, a_s, a_r, z_s, z_r, y_s, y_r, c_s, c_r, h_s, h_r, hc_s, hc_r, o_s, o_r,
 ):
     ctx = lax.axis_index("ctx")
@@ -90,7 +88,8 @@
         return cp
 
     own_tok = move(tok_in, tok.at[0], loc_sem.at[0])
-    own_open = move(opened, opens.at[0], loc_sem.at[1])
+    own_tab = move(tab_in, tab, loc_sem.at[1])
+    own_starts = move(starts_in, starts, loc_sem.at[6])
     row16 = c * 64 + y * 16
     parts = ((wk_in, HD, 0), (wv_in, HD, HD), (wq_in, QC, 2 * HD))
     own_w = [
@@ -105,6 +104,9 @@
     barrier = pltpu.get_barrier_semaphore()
     for peer in peers:
         pl.semaphore_signal(barrier, inc=1, device_id=peer, device_id_type=MESH)
+    for k in range(REACH):
+        opens[0, :, k * ROWS:(k + 1) * ROWS] = jnp.full((1, ROWS), crossing[0, 0, REACH - 1 - k], jnp.int32)
+    opens[0, :, REACH * ROWS:] = jnp.ones((1, ROWS), jnp.int32)
     pl.semaphore_wait(barrier, len(peers))
 
     for i, (ref, n, at) in enumerate(parts):
@@ -125,7 +127,7 @@
             )
     for k in (1, 3, 2):
         slot = SLOT_OF[(-k) % NX]
-        send(opened, opens.at[slot], a_s.at[3, k - 1], a_r.at[3, slot - 1], dev(xs(k), y, z, c))
+        send(opens.at[0], opens.at[slot], a_s.at[3, k - 1], a_r.at[3, slot - 1], dev(xs(k), y, z, c))
 
     groups = ((0, 2 * HD), (2 * HD, QC))
 
@@ -193,38 +195,43 @@
             send(tok.at[slot, :, cols], tok.at[3, :, cols], tok_s.at[2, n], tok_r.at[2, n], dev(xs(k), y, z, c))
 
     stage_z(0)
+    stage_y(0)
     stage_z(1)
-    stage_y(0)
     forward_tokens(0)
     stage_forward(0)
     forward_tokens(1)
+    stage_share(0)
     stage_y(1)
-    stage_share(0)
-    stage_forward(1)
     stage_end(0)
-    for side, slot in enumerate((2, 1)):
-        for n in (2 - 2 * side, 3 - 2 * side):
-            cols = pl.ds(n * CH, CH)
-            arrive(tok.at[slot, :, cols], tok_s.at[side, n], tok_r.at[slot - 1, n])
+
+    def side_tokens():
+        for side, slot in enumerate((2, 1)):
+            for n in (2 - 2 * side, 3 - 2 * side):
+                cols = pl.ds(n * CH, CH)
+                arrive(tok.at[slot, :, cols], tok_s.at[side, n], tok_r.at[slot - 1, n])
+
     own_tok.wait()
-
-    cos_row, sin_row = row_tab[0], row_tab[1]
+    own_tab.wait()
+    own_starts.wait()
+    cos_row, sin_row = tab[0, 0:ROWS], tab[1, 0:ROWS]
     sign = jnp.where(lax.broadcasted_iota(jnp.int32, (1, HD), 1) < HD // 2, -1.0, 1.0).astype(jnp.float32)
 
     def shard_of(p):
         return xs(OFFSETS[p]) * (2 * NZ) + z * 2 + c
 
     def rotary(p):
-        tab = shard_tab[shard_of(p)]
-        ca, sa = tab[0:1, :], tab[1:2, :]
+        ca = tab[0, pl.ds(ROWS + shard_of(p), 1)]
+        sa = tab[1, pl.ds(ROWS + shard_of(p), 1)]
         return ca * cos_row - sa * sin_row, (sa * cos_row + ca * sin_row) * sign
 
     def rotate(v, cs, sn):
         return v * cs + pltpu.roll(v, HD // 2, 1) * sn
 
-    def project(first, count, at, n):
+    def project(first, count, at, n, ready=None):
         total = None
-        for j in range(4):
+        for j in (0, 2, 1, 3):
+            if ready is not None:
+                ready(j)
             rows = tok[first:first + count, :, j * CH:(j + 1) * CH].reshape(count * ROWS, CH)
             cols = w[j, :, :, at:at + n].reshape(CH, n)
             part = jnp.dot(rows, cols, preferred_element_type=jnp.float32)
@@ -234,7 +241,10 @@
     wrap = jnp.where(z == NZ - 1, 1, 0)
 
     def slot_ahead(p):
-        turned = SLOT_OF[(OFFSETS[p] + 1) % NX]
+        if isinstance(p, int):
+            turned = SLOT_OF[(OFFSETS[p] + 1) % NX]
+        else:
+            turned = jnp.where(p == 2, SLOT_OF[(OFFSETS[2] + 1) % NX], SLOT_OF[(OFFSETS[3] + 1) % NX])
         return jnp.where(wrap == 1, turned, p)
 
     def send_own(p):
@@ -243,8 +253,8 @@
         n = slot_ahead(p)
         send(tile, kv.at[n, 6 + c], h_s.at[p, 0], h_r.at[n, 0], dev(x, y, zs(1), c))
 
-    def keys(first, count):
-        total = project(first, count, 0, 2 * HD)
+    def keys(first, count, ready=None):
+        total = project(first, count, 0, 2 * HD, ready)
         for i in range(count):
             p = first + i
             part = total[i * ROWS:(i + 1) * ROWS]
@@ -294,7 +304,8 @@
     def attend(p):
         s = shard_of(p)
         q_at = (s * ROWS + lax.broadcasted_iota(jnp.int32, (ROWS, 1), 0)).astype(jnp.float32)
-        begin = jnp.max(jnp.where(starts[...] <= q_at, starts[...], 0.0), axis=1, keepdims=True)
+        first = starts[...].astype(jnp.float32)
+        begin = jnp.max(jnp.where(first <= q_at, first, 0.0), axis=1, keepdims=True)
         k_at = ((s - REACH) * ROWS + lax.broadcasted_iota(jnp.int32, (1, WINDOW), 1)).astype(jnp.float32)
         k_at = jnp.where(opens[p] == 1, k_at, -1.0)
         seen = (k_at <= q_at) & (k_at >= begin)
@@ -317,25 +328,38 @@
         else:
             send(att.at[p], mine, o_s.at[k - 1], o_r.at[k - 1], dev(xs(k), y, z, c))
 
-    keys(0, 3)
+    def last_tokens(j):
+        arrive(tok.at[3, :, pl.ds(j * CH, CH)], tok_s.at[2, j], tok_r.at[2, j])
+
+    def early(d):
+        for p in (0, 1, jnp.where(z < d, 3, 2)):
+            pass_on(p, d)
+
+    def late(d):
+        pass_on(jnp.where(z < d, 2, 3), d)
+
+    keys(0, 1)
+    side_tokens()
+    keys(1, 2)
+    early(1)
+    stage_forward(1)
+    early(2)
+    keys(3, 1, last_tokens)
+    late(1)
+    early(3)
     stage_share(1)
-    for j in range(4):
-        cols = pl.ds(j * CH, CH)
-        arrive(tok.at[3, :, cols], tok_s.at[2, j], tok_r.at[2, j])
-    keys(3, 1)
+    late(2)
     stage_end(1)
-    for p in (0, 1):
-        for d in (1, 2, 3):
-            pass_on(p, d)
     queries(0, 3)
-    for p in (2, 3):
-        for d in (1, 2, 3):
-            pass_on(p, d)
-    queries(3, 1)
-    own_open.wait()
     for slot in (1, 2, 3):
         arrive(opens.at[slot], a_s.at[3, slot - 1], a_r.at[3, slot - 1])
-    for p in (1, 0, 2, 3):
+    late(3)
+    gather_keys(1)
+    attend(1)
+    queries(3, 1)
+    gather_keys(0)
+    attend(0)
+    for p in (2, 3):
         gather_keys(p)
         attend(p)
 
@@ -352,19 +376,13 @@
 
 
 def local(tokens, w_query, w_key, w_value, doc_starts, crossing):
-    row_tab, shard_tab = tables()
-    starts = jnp.pad(doc_starts, ((0, 0), (0, HD - doc_starts.shape[1])), constant_values=NX * NZ * 2 * ROWS)
-    starts = starts.astype(jnp.float32)
-    opened = jnp.concatenate([crossing[0, :, ::-1], jnp.ones((1, 1), jnp.int32)], axis=1)
-    opened = jnp.repeat(opened, ROWS, axis=1)
     anyw = pl.BlockSpec(memory_space=pl.ANY)
-    vmem = pl.BlockSpec(memory_space=pltpu.VMEM)
     dma = pltpu.SemaphoreType.DMA
     bf16 = jnp.bfloat16
     out = pl.pallas_call(
         kernel,
         out_shape=jax.ShapeDtypeStruct((ROWS, NX * QC), bf16),
-        in_specs=[anyw, anyw, anyw, anyw, vmem, vmem, vmem, vmem],
+        in_specs=[anyw, anyw, anyw, anyw, anyw, pl.BlockSpec(memory_space=pltpu.SMEM), anyw],
         out_specs=anyw,
         scratch_shapes=[
             pltpu.VMEM((4, ROWS, D), bf16),
@@ -373,7 +391,9 @@
             pltpu.VMEM((4, GROUP, ROWS, HD), bf16),
             pltpu.VMEM((4, ROWS, QC), bf16),
             pltpu.VMEM((4, 1, WINDOW), jnp.int32),
-            dma((6,)),
+            pltpu.VMEM((2, ROWS + NX * NZ * 2, HD), jnp.float32),
+            pltpu.VMEM(doc_starts.shape, jnp.int32),
+            dma((7,)),
             dma((3, 4)), dma((3, 4)),
             dma((4, 3)), dma((4, 3)),
             dma((2, 7)), dma((2, 7)),
@@ -384,11 +404,10 @@
             dma((3,)), dma((3,)),
         ],
         compiler_params=pltpu.CompilerParams(
-            collective_id=0, has_side_effects=True, vmem_limit_bytes=48 << 20
+            collective_id=0, has_side_effects=True, vmem_limit_bytes=62 << 20
         ),
     )(
-        tokens.reshape(ROWS, D), w_query, w_key, w_value, starts, opened,
-        jnp.asarray(row_tab), jnp.asarray(shard_tab),
+        tokens.reshape(ROWS, D), w_query, w_key, w_value, doc_starts, crossing, jnp.asarray(tables()),
     )
     return out.reshape(1, ROWS, NX * QC)
 

time: 118 us -> 75.4 us (0.64)
  the two profiles are of different devices: /device:TPU:192 before, /device:TPU:35 now
where the time goes in v2:
time: 75.4 us; the launch traced here: 75.3 us
  Pallas kernels  73.4 us (97%)
  local copies, waits for them, and re-layouts  1.88 us (2%)
    pallas_call x1, Pallas kernels, local(): pl.pallas_call(kernel, out_shape=jax.ShapeDtypeStruct((ROWS, NX * QC), bf...  73.4 us
    unnamed x1, local copies, waits for them, and re-layouts  1.88 us

profile of v2, /device:TPU:35, one launch (start us, length us, event | category | flops | bytes accessed | tf_op | source)
XLA Modules:
  0.0 75.3 jit_solution(1670146625761683488)
XLA Ops:
  0.0 73.4 %shard_map.73 = bf16[128,2048]{1,0:T(8,128)(2,1)} custom-call(bf16[128,4096]{1,0:T(8,128)(2,1)} %bitcast.3, bf16[16,2048]{1,0:T(8,128)(2,1)} %wq_in.1, bf16[16,512]{1,0:T(8,128)(2,1)} %wk_in.1, bf16[16,512]{1,0:T(8,128)(2,1)} %wv_in.1, s32[1,71]{1,0:T(1,128)} %starts_in.1, s32[1,1,7]{2,1,0:T(1,128)} %crossing.1, f32[2,192,128]{2,1,0:T(8,128)} %constant.2.clone.tab_in), custom_call_target="tpu_custom_call" | custom-call | tf_op jit(solution)/shard_map/pallas_call | solution.py:382
  73.4 1.9 %copy.9 = bf16[1,128,2048]{2,1,0:T(8,128)(2,1)} copy(bf16[1,128,2048]{2,1,0:T(8,128)(2,1)} %bitcast.2) | data formatting | bytes 1048576
